TPU v7x, 256 devices: a whole 4x4x8 slice. The times are simulated.
256 devices in a mesh: dp: 128 (over z, x, y), pair: 2 (over core).
Axes of the slice: x: 4, y: 4, z: 8, core: 2. Of those that a mesh axis runs over, the one named last changes fastest.
Arguments:
- hidden_in: bfloat16 [32768, 1536], P(('dp', 'pair')), may hold values from -24 to 24
- segment_ids: int32 [32768], replicated, may hold values from 0 to 511, as said below
- frame_mask: int32 [32768], P(('dp', 'pair')), may hold values from 0 to 1, as said below
- dw_kernel: float32 [31, 1536], P(None, ('dp', 'pair')), may hold values from -1 to 1
- norm_scale: float32 [1536], P(('dp', 'pair')), may hold values from 0.1 to 1.9
- norm_shift: float32 [1536], P(('dp', 'pair')), may hold values from -3 to 3
- out_weight: bfloat16 [1536, 1536], P(('dp', 'pair')), may hold values from -0.15625 to 0.15625
- cotangent: bfloat16 [32768, 1536], P(('dp', 'pair')), may hold values from -6 to 6
Outputs:
- module_out: bfloat16 [32768, 1536], P(('dp', 'pair'))
- grad_hidden: bfloat16 [32768, 1536], P(('dp', 'pair'))
- grad_kernel: float32 [31, 1536], P(None, ('dp', 'pair'))
- grad_scale: float32 [1536], P(('dp', 'pair'))
- grad_shift: float32 [1536], P(('dp', 'pair'))
- grad_weight: float32 [1536, 1536], P(('dp', 'pair'))
Inputs may be any that keep to these rules, and one draw needn't show every extreme that they name: `segment_ids`: non-falling along the stream, starting at 0; each utterance has 1 to 192 frames; no utterance begins at a frame whose index is a positive multiple of 128. `frame_mask`: 1 on every frame whose index modulo 16 is 0 or 15.
All inputs are finite; a program needn't handle non-finite values.
Results may differ from a plain program's by a relative error of at most 0.0049.
Values may be sent and summed in bfloat16 or wider, within the bound.
No kernel may reach another device: no remote copies, remote signals or barrier semaphores. Data moves between devices by JAX's collectives and lax.ppermute only.
A program may use at most 128 MiB of HBM per device.

v0:
```python
import jax
import jax.numpy as jnp
from jax import lax
from jax.sharding import PartitionSpec as P

KERNEL = 31


def padded(cells, sides, width):
    for axis, dim in sides:
        count = lax.axis_size(axis)
        ends = count - 1
        head = lax.slice_in_dim(cells, 0, width, axis=dim)
        tail = lax.slice_in_dim(cells, cells.shape[dim] - width, cells.shape[dim], axis=dim)
        cells = jnp.concatenate(
            [
                lax.ppermute(tail, axis, [(i, (i + 1) % count) for i in range(ends)]),
                cells,
                lax.ppermute(head, axis, [((i + 1) % count, i) for i in range(ends)]),
            ],
            axis=dim,
        )
    return cells


def local(
    hidden_in, segment_ids, frame_mask, dw_kernel, norm_scale, norm_shift, out_weight, cotangent
):
    local_rows = hidden_in.shape[0]
    shard_cols = norm_scale.shape[0]
    half = KERNEL // 2
    device_pos = lax.axis_index(("dp", "pair"))
    weight_col = frame_mask.astype(jnp.float32)[:, None]
    stacked = jnp.concatenate([dw_kernel, norm_scale[None, :], norm_shift[None, :]], axis=0)
    params_full = lax.all_gather(stacked, ("dp", "pair"), axis=1, tiled=True)
    kernel_full = params_full[:KERNEL]
    scale_full = params_full[KERNEL]
    shift_full = params_full[KERNEL + 1]
    seg_pad = jnp.pad(segment_ids, (half, half), constant_values=-1)
    seg_local = lax.dynamic_slice_in_dim(seg_pad, device_pos * local_rows, local_rows + 2 * half)
    own_seg = seg_local[half : half + local_rows]
    masked = jnp.where(frame_mask[:, None] == 1, hidden_in, jnp.zeros_like(hidden_in))
    padded_in = padded(masked, ((("dp", "pair"), 0),), half).astype(jnp.float32)
    conv = jnp.zeros((local_rows, params_full.shape[1]), jnp.float32)
    for offset in range(KERNEL):
        same_seg = (seg_local[offset : offset + local_rows] == own_seg)[:, None]
        conv = conv + jnp.where(
            same_seg, kernel_full[offset] * padded_in[offset : offset + local_rows], 0.0
        )
    total, count = lax.psum(
        (jnp.sum(weight_col * conv, axis=0), jnp.sum(weight_col)), ("dp", "pair")
    )
    mean = total / count
    centred = conv - mean
    spread = lax.psum(jnp.sum(weight_col * centred * centred, axis=0), ("dp", "pair"))
    variance = spread / count
    inv_std = lax.rsqrt(variance + 1e-05)
    normed = centred * inv_std
    pre = scale_full * normed + shift_full
    sig = jax.nn.sigmoid(pre)
    act = (weight_col * pre * sig).astype(jnp.bfloat16)
    weight_full = lax.all_gather(out_weight, ("dp", "pair"), axis=0, tiled=True)
    module_out = jnp.dot(act, weight_full, preferred_element_type=jnp.float32).astype(jnp.bfloat16)
    grad_act = lax.dot_general(
        cotangent, weight_full, (((1,), (1,)), ((), ())), preferred_element_type=jnp.float32
    )
    grad_pre = weight_col * grad_act * sig * (1.0 + pre * (1.0 - sig))
    scale_sum, shift_sum = lax.psum(
        (jnp.sum(grad_pre * normed, axis=0), jnp.sum(grad_pre, axis=0)), ("dp", "pair")
    )
    col_start = device_pos * shard_cols
    grad_scale = lax.dynamic_slice_in_dim(scale_sum, col_start, shard_cols)
    grad_shift = lax.dynamic_slice_in_dim(shift_sum, col_start, shard_cols)
    grad_conv = (
        weight_col
        * scale_full
        * inv_std
        * (grad_pre - shift_sum / count - normed * scale_sum / count)
    )
    grad_pad = padded(grad_conv, ((("dp", "pair"), 0),), half)
    grad_local = jnp.zeros_like(grad_conv)
    tap_rows = []
    for offset in range(KERNEL):
        same_fwd = (seg_local[offset : offset + local_rows] == own_seg)[:, None]
        tap_rows.append(
            jnp.sum(
                jnp.where(same_fwd, grad_conv * padded_in[offset : offset + local_rows], 0.0),
                axis=0,
            )
        )
        back = 2 * half - offset
        same_back = (seg_local[back : back + local_rows] == own_seg)[:, None]
        grad_local = grad_local + jnp.where(
            same_back, kernel_full[offset] * grad_pad[back : back + local_rows], 0.0
        )
    grad_kernel = lax.psum_scatter(
        jnp.stack(tap_rows, axis=0), ("dp", "pair"), scatter_dimension=1, tiled=True
    )
    grad_hidden = (weight_col * grad_local).astype(jnp.bfloat16)
    grad_weight = lax.psum_scatter(
        lax.dot_general(
            act, cotangent, (((0,), (0,)), ((), ())), preferred_element_type=jnp.float32
        ),
        ("dp", "pair"),
        scatter_dimension=0,
        tiled=True,
    )
    return (module_out, grad_hidden, grad_kernel, grad_scale, grad_shift, grad_weight)


def solution(mesh):
    return jax.shard_map(
        local,
        mesh=mesh,
        in_specs=(
            P(("dp", "pair"), None),
            P(),
            P(("dp", "pair")),
            P(None, ("dp", "pair")),
            P(("dp", "pair")),
            P(("dp", "pair")),
            P(("dp", "pair"), None),
            P(("dp", "pair"), None),
        ),
        out_specs=(
            P(("dp", "pair"), None),
            P(("dp", "pair"), None),
            P(None, ("dp", "pair")),
            P(("dp", "pair")),
            P(("dp", "pair")),
            P(("dp", "pair"), None),
        ),
        check_vma=False,
    )
```

profile of v0, /device:TPU:1, one launch (start us, length us, event | category | flops | bytes accessed | tf_op | source)
XLA Modules:
  0.0 1933.7 jit_solution(4667449494425731221)
XLA Ops:
  9.7 4.6 collective-permute-start
  19.3 68.0 %all-gather = f32[256,6,33]{2,1,0:T(8,128)S(1)} all-gather(f32[1,6,33]{2,1,0:T(8,128)S(1)} %maximum_bitcast_fusion), channel_id=1, replica_groups=mesh['dp'=128,'pair'=2] {'dp','pair'}, dimensions={0}, use_global_device_ids=true | all-gather | bytes 203544 | tf_op jit(solution)/shard_map/all_gather | solution.py:35
  88.0 5.6 slice_reduce_fusion.31
  93.6 8.2 slice_reduce_fusion.32
  102.8 4.6 multiply_reduce_fusion.2
  107.4 75.7 %all-reduce.5 = (f32[1536]{0:T(1024)S(1)}, f32[]{:T(128)}) all-reduce(f32[1536]{0:T(1024)S(1)} %get-tuple-element.89, f32[]{:T(128)} %convert_reduce_fusion), channel_id=1, replica_groups=mesh['dp'=128,'pair'=2] {'dp','pair'}, use_global_device_ids=true, to_apply=%region_1.2 | all-reduce | flops 1537 | bytes 12296 | tf_op jit(solution)/shard_map/psum | solution.py:50
  184.0 74.2 %psum.37 = f32[1536]{0:T(1024)S(1)} all-reduce(f32[1536]{0:T(1024)S(1)} %fusion.119), channel_id=1, replica_groups=mesh['dp'=128,'pair'=2] {'dp','pair'}, use_global_device_ids=true, to_apply=%region_5.6 | all-reduce | flops 1536 | bytes 12288 | tf_op jit(solution)/shard_map/psum | solution.py:55
  258.9 5.2 fusion.124
  264.0 709.9 %fusion = f32[8,1536]{1,0:T(8,128)S(1)} fusion(f32[1536,1536]{1,0:T(8,128)} %fusion.124), kind=kCustom, calls=%all-reduce-scatter | all-reduce-scatter fusion | flops 3145729 | bytes 9486336
  978.8 11.0 collective-permute-start.67
  1005.7 17.9 collective-permute-start.51
  1060.5 6.1 collective-permute-start.35
  1066.6 13.1 collective-permute-start.34
  1079.7 13.1 collective-permute-start.33
  1092.9 13.1 collective-permute-start.32
  1106.0 13.1 collective-permute-start.31
  1119.2 13.1 collective-permute-start.30
  1132.3 13.1 collective-permute-start.29
  1145.5 13.1 collective-permute-start.28
  1158.6 13.1 collective-permute-start.27
  1171.8 13.1 collective-permute-start.26
  1184.9 13.1 collective-permute-start.25
  1198.1 13.1 collective-permute-start.24
  1211.2 13.1 collective-permute-start.23
  1224.4 13.1 collective-permute-start.22
  1237.5 13.1 collective-permute-start.21
  1250.7 13.1 collective-permute-start.20
  1263.8 13.1 collective-permute-start.19
  1277.0 13.1 collective-permute-start.18
  1290.1 13.1 collective-permute-start.17
  1303.3 13.1 collective-permute-start.16
  1316.4 13.3 collective-permute-start.15
  1329.7 13.1 collective-permute-start.14
  1342.9 13.1 collective-permute-start.13
  1356.0 13.1 collective-permute-start.12
  1369.2 13.1 collective-permute-start.11
  1382.3 13.1 collective-permute-start.10
  1395.5 13.1 collective-permute-start.9
  1408.6 13.7 collective-permute-start.8
  1422.4 13.1 collective-permute-start.7
  1435.5 13.1 collective-permute-start.6
  1448.7 13.1 collective-permute-start.5
  1466.0 97.2 %concatenate.45 = f32[518,1536]{1,0:T(8,128)} concatenate(f32[6,1536]{1,0:T(8,128)S(1)} %collective-permute-done.67, f32[8,1536]{1,0:T(8,128)S(1)} %collective-permute-done.66, f32[8,1536]{1,0:T(8,128)S(1)} %collective-permute-done.65, f32[8,1536]{1,0:T(8,128)S(1)} %collective-permute-done.64, f32[8,1536]{1,0:T(8,128)S(1)} %collective-permute-done.63, ...), dimensions={0} | concatenate | bytes 6365184
  1564.7 8.4 reshape.52
  1573.1 4.1 convolution_convert_fusion
  1580.0 79.5 %all-reduce.4 = (f32[1536]{0:T(1024)S(1)}, f32[1536]{0:T(1024)S(1)}) all-reduce(f32[1536]{0:T(1024)S(1)} %get-tuple-element.50, f32[1536]{0:T(1024)S(1)} %get-tuple-element.49), channel_id=1, replica_groups=mesh['dp'=128,'pair'=2] {'dp','pair'}, use_global_device_ids=true, to_apply=%region_9.10 | all-reduce | flops 3072 | bytes 24576 | tf_op jit(solution)/shard_map/psum | solution.py:68
  1678.1 9.9 fusion.9
  1688.0 237.1 %all-reduce.8.cloned.1.call-done = f32[31,1536]{1,0:T(8,128)} async-done(((f32[31,1536]{1,0:T(8,128)}), f32[31,1536]{1,0:T(8,128)}) %all-reduce.8.cloned.1.call-update) | async-done | bytes 190480
  (346 shorter events, 94.8 us)
Async XLA Ops:
  7.2 1557.6 %all-gather.4.cloned.1.call-start = ((), (), s32[]{:S(2)}) async-start(), calls=%async_computation | async-start | bytes 6316032 | tf_op jit(solution)/shard_map/all_gather | solution.py:62
  7.9 1917.2 %all-reduce.8.cloned.1.call-start = ((), (), s32[]{:S(2)}) async-start(), calls=%async_computation.1 | async-start | bytes 393216
  9.7 92.7 %collective-permute-start = (bf16[15,1536]{1,0:T(8,128)(2,1)S(1)}, bf16[15,1536]{1,0:T(8,128)(2,1)S(1)}, u32[]{:S(2)}, u32[]{:S(2)}) collective-permute-start(bf16[15,1536]{1,0:T(8,128)(2,1)S(1)} %get-tuple-element.93), channel_id=1, source_target_pairs={{0,1},{1,2},{2,3},{3,4},{4,5},{5,6},{6,7},{7,8},{8,9},{9,10},{10,1... | collective-permute-start | bytes 138248 | tf_op jit(solution)/shard_map/ppermute | solution.py:17
  14.3 88.1 %collective-permute-start.1 = (bf16[15,1536]{1,0:T(8,128)(2,1)S(1)}, bf16[15,1536]{1,0:T(8,128)(2,1)S(1)}, u32[]{:S(2)}, u32[]{:S(2)}) collective-permute-start(bf16[15,1536]{1,0:T(8,128)(2,1)S(1)} %get-tuple-element.94), channel_id=1, source_target_pairs={{1,0},{2,1},{3,2},{4,3},{5,4},{6,5},{7,6},{8,7},{9,8},{10,9},{11,1... | collective-permute-start | bytes 138248 | tf_op jit(solution)/shard_map/ppermute | solution.py:19
  974.0 18.7 collective-permute-start.66
  975.3 18.7 collective-permute-start.65
  977.5 17.8 collective-permute-start.64
  1000.5 23.2 %collective-permute-start.55 = (f32[8,1536]{1,0:T(8,128)S(1)}, f32[8,1536]{1,0:T(8,128)S(1)}, u32[]{:S(2)}, u32[]{:S(2)}) collective-permute-start(f32[8,1536]{1,0:T(8,128)S(1)} %fusion), channel_id=1, source_target_pairs={{0,52},{1,53},{2,54},{3,55},{4,56},{5,57},{6,58},{7,59},{8,60},{9,... | collective-permute-start | bytes 147464
  1001.8 25.0 %collective-permute-start.54 = (f32[8,1536]{1,0:T(8,128)S(1)}, f32[8,1536]{1,0:T(8,128)S(1)}, u32[]{:S(2)}, u32[]{:S(2)}) collective-permute-start(f32[8,1536]{1,0:T(8,128)S(1)} %fusion), channel_id=1, source_target_pairs={{0,51},{1,52},{2,53},{3,54},{4,55},{5,56},{6,57},{7,58},{8,59},{9,... | collective-permute-start | bytes 147464
  1003.1 25.3 %collective-permute-start.53 = (f32[8,1536]{1,0:T(8,128)S(1)}, f32[8,1536]{1,0:T(8,128)S(1)}, u32[]{:S(2)}, u32[]{:S(2)}) collective-permute-start(f32[8,1536]{1,0:T(8,128)S(1)} %fusion), channel_id=1, source_target_pairs={{0,50},{1,51},{2,52},{3,53},{4,54},{5,55},{6,56},{7,57},{8,58},{9,... | collective-permute-start | bytes 147464
  1004.4 26.9 %collective-permute-start.52 = (f32[8,1536]{1,0:T(8,128)S(1)}, f32[8,1536]{1,0:T(8,128)S(1)}, u32[]{:S(2)}, u32[]{:S(2)}) collective-permute-start(f32[8,1536]{1,0:T(8,128)S(1)} %fusion), channel_id=1, source_target_pairs={{0,49},{1,50},{2,51},{3,52},{4,53},{5,54},{6,55},{7,56},{8,57},{9,... | collective-permute-start | bytes 147464
  1005.7 29.5 %collective-permute-start.51 = (f32[8,1536]{1,0:T(8,128)S(1)}, f32[8,1536]{1,0:T(8,128)S(1)}, u32[]{:S(2)}, u32[]{:S(2)}) collective-permute-start(f32[8,1536]{1,0:T(8,128)S(1)} %fusion), channel_id=1, source_target_pairs={{0,48},{1,49},{2,50},{3,51},{4,52},{5,53},{6,54},{7,55},{8,56},{9,... | collective-permute-start | bytes 147464
  1023.7 15.5 collective-permute-start.50
  1048.6 18.0 collective-permute-start.39
  1052.3 27.5 %collective-permute-start.38 = (f32[8,1536]{1,0:T(8,128)S(1)}, f32[8,1536]{1,0:T(8,128)S(1)}, u32[]{:S(2)}, u32[]{:S(2)}) collective-permute-start(f32[8,1536]{1,0:T(8,128)S(1)} %fusion), channel_id=1, source_target_pairs={{0,35},{1,36},{2,37},{3,38},{4,39},{5,40},{6,41},{7,42},{8,43},{9,... | collective-permute-start | bytes 147464
  1054.7 38.1 %collective-permute-start.37 = (f32[8,1536]{1,0:T(8,128)S(1)}, f32[8,1536]{1,0:T(8,128)S(1)}, u32[]{:S(2)}, u32[]{:S(2)}) collective-permute-start(f32[8,1536]{1,0:T(8,128)S(1)} %fusion), channel_id=1, source_target_pairs={{0,34},{1,35},{2,36},{3,37},{4,38},{5,39},{6,40},{7,41},{8,42},{9,... | collective-permute-start | bytes 147464
  1058.9 47.2 %collective-permute-start.36 = (f32[8,1536]{1,0:T(8,128)S(1)}, f32[8,1536]{1,0:T(8,128)S(1)}, u32[]{:S(2)}, u32[]{:S(2)}) collective-permute-start(f32[8,1536]{1,0:T(8,128)S(1)} %fusion), channel_id=1, source_target_pairs={{0,33},{1,34},{2,35},{3,36},{4,37},{5,38},{6,39},{7,40},{8,41},{9,... | collective-permute-start | bytes 147464
  1060.5 58.7 %collective-permute-start.35 = (f32[8,1536]{1,0:T(8,128)S(1)}, f32[8,1536]{1,0:T(8,128)S(1)}, u32[]{:S(2)}, u32[]{:S(2)}) collective-permute-start(f32[8,1536]{1,0:T(8,128)S(1)} %fusion), channel_id=1, source_target_pairs={{0,32},{1,33},{2,34},{3,35},{4,36},{5,37},{6,38},{7,39},{8,40},{9,... | collective-permute-start | bytes 147464
  1066.6 65.7 %collective-permute-start.34 = (f32[8,1536]{1,0:T(8,128)S(1)}, f32[8,1536]{1,0:T(8,128)S(1)}, u32[]{:S(2)}, u32[]{:S(2)}) collective-permute-start(f32[8,1536]{1,0:T(8,128)S(1)} %fusion), channel_id=1, source_target_pairs={{0,31},{1,32},{2,33},{3,34},{4,35},{5,36},{6,37},{7,38},{8,39},{9,... | collective-permute-start | bytes 147464
  1079.7 65.7 %collective-permute-start.33 = (f32[8,1536]{1,0:T(8,128)S(1)}, f32[8,1536]{1,0:T(8,128)S(1)}, u32[]{:S(2)}, u32[]{:S(2)}) collective-permute-start(f32[8,1536]{1,0:T(8,128)S(1)} %fusion), channel_id=1, source_target_pairs={{0,30},{1,31},{2,32},{3,33},{4,34},{5,35},{6,36},{7,37},{8,38},{9,... | collective-permute-start | bytes 147464
  1092.9 65.7 %collective-permute-start.32 = (f32[8,1536]{1,0:T(8,128)S(1)}, f32[8,1536]{1,0:T(8,128)S(1)}, u32[]{:S(2)}, u32[]{:S(2)}) collective-permute-start(f32[8,1536]{1,0:T(8,128)S(1)} %fusion), channel_id=1, source_target_pairs={{0,29},{1,30},{2,31},{3,32},{4,33},{5,34},{6,35},{7,36},{8,37},{9,... | collective-permute-start | bytes 147464
  1106.0 65.7 %collective-permute-start.31 = (f32[8,1536]{1,0:T(8,128)S(1)}, f32[8,1536]{1,0:T(8,128)S(1)}, u32[]{:S(2)}, u32[]{:S(2)}) collective-permute-start(f32[8,1536]{1,0:T(8,128)S(1)} %fusion), channel_id=1, source_target_pairs={{0,28},{1,29},{2,30},{3,31},{4,32},{5,33},{6,34},{7,35},{8,36},{9,... | collective-permute-start | bytes 147464
  1119.2 65.7 %collective-permute-start.30 = (f32[8,1536]{1,0:T(8,128)S(1)}, f32[8,1536]{1,0:T(8,128)S(1)}, u32[]{:S(2)}, u32[]{:S(2)}) collective-permute-start(f32[8,1536]{1,0:T(8,128)S(1)} %fusion), channel_id=1, source_target_pairs={{0,27},{1,28},{2,29},{3,30},{4,31},{5,32},{6,33},{7,34},{8,35},{9,... | collective-permute-start | bytes 147464
  1132.3 65.7 %collective-permute-start.29 = (f32[8,1536]{1,0:T(8,128)S(1)}, f32[8,1536]{1,0:T(8,128)S(1)}, u32[]{:S(2)}, u32[]{:S(2)}) collective-permute-start(f32[8,1536]{1,0:T(8,128)S(1)} %fusion), channel_id=1, source_target_pairs={{0,26},{1,27},{2,28},{3,29},{4,30},{5,31},{6,32},{7,33},{8,34},{9,... | collective-permute-start | bytes 147464
  1145.5 65.7 %collective-permute-start.28 = (f32[8,1536]{1,0:T(8,128)S(1)}, f32[8,1536]{1,0:T(8,128)S(1)}, u32[]{:S(2)}, u32[]{:S(2)}) collective-permute-start(f32[8,1536]{1,0:T(8,128)S(1)} %fusion), channel_id=1, source_target_pairs={{0,25},{1,26},{2,27},{3,28},{4,29},{5,30},{6,31},{7,32},{8,33},{9,... | collective-permute-start | bytes 147464
  1158.6 65.7 %collective-permute-start.27 = (f32[8,1536]{1,0:T(8,128)S(1)}, f32[8,1536]{1,0:T(8,128)S(1)}, u32[]{:S(2)}, u32[]{:S(2)}) collective-permute-start(f32[8,1536]{1,0:T(8,128)S(1)} %fusion), channel_id=1, source_target_pairs={{0,24},{1,25},{2,26},{3,27},{4,28},{5,29},{6,30},{7,31},{8,32},{9,... | collective-permute-start | bytes 147464
  1171.8 65.7 %collective-permute-start.26 = (f32[8,1536]{1,0:T(8,128)S(1)}, f32[8,1536]{1,0:T(8,128)S(1)}, u32[]{:S(2)}, u32[]{:S(2)}) collective-permute-start(f32[8,1536]{1,0:T(8,128)S(1)} %fusion), channel_id=1, source_target_pairs={{0,23},{1,24},{2,25},{3,26},{4,27},{5,28},{6,29},{7,30},{8,31},{9,... | collective-permute-start | bytes 147464
  1184.9 65.7 %collective-permute-start.25 = (f32[8,1536]{1,0:T(8,128)S(1)}, f32[8,1536]{1,0:T(8,128)S(1)}, u32[]{:S(2)}, u32[]{:S(2)}) collective-permute-start(f32[8,1536]{1,0:T(8,128)S(1)} %fusion), channel_id=1, source_target_pairs={{0,22},{1,23},{2,24},{3,25},{4,26},{5,27},{6,28},{7,29},{8,30},{9,... | collective-permute-start | bytes 147464
  1198.1 65.7 %collective-permute-start.24 = (f32[8,1536]{1,0:T(8,128)S(1)}, f32[8,1536]{1,0:T(8,128)S(1)}, u32[]{:S(2)}, u32[]{:S(2)}) collective-permute-start(f32[8,1536]{1,0:T(8,128)S(1)} %fusion), channel_id=1, source_target_pairs={{0,21},{1,22},{2,23},{3,24},{4,25},{5,26},{6,27},{7,28},{8,29},{9,... | collective-permute-start | bytes 147464
  1211.2 65.7 %collective-permute-start.23 = (f32[8,1536]{1,0:T(8,128)S(1)}, f32[8,1536]{1,0:T(8,128)S(1)}, u32[]{:S(2)}, u32[]{:S(2)}) collective-permute-start(f32[8,1536]{1,0:T(8,128)S(1)} %fusion), channel_id=1, source_target_pairs={{0,20},{1,21},{2,22},{3,23},{4,24},{5,25},{6,26},{7,27},{8,28},{9,... | collective-permute-start | bytes 147464
  1224.4 65.7 %collective-permute-start.22 = (f32[8,1536]{1,0:T(8,128)S(1)}, f32[8,1536]{1,0:T(8,128)S(1)}, u32[]{:S(2)}, u32[]{:S(2)}) collective-permute-start(f32[8,1536]{1,0:T(8,128)S(1)} %fusion), channel_id=1, source_target_pairs={{0,19},{1,20},{2,21},{3,22},{4,23},{5,24},{6,25},{7,26},{8,27},{9,... | collective-permute-start | bytes 147464
  1237.5 65.7 %collective-permute-start.21 = (f32[8,1536]{1,0:T(8,128)S(1)}, f32[8,1536]{1,0:T(8,128)S(1)}, u32[]{:S(2)}, u32[]{:S(2)}) collective-permute-start(f32[8,1536]{1,0:T(8,128)S(1)} %fusion), channel_id=1, source_target_pairs={{0,18},{1,19},{2,20},{3,21},{4,22},{5,23},{6,24},{7,25},{8,26},{9,... | collective-permute-start | bytes 147464
  1250.7 65.7 %collective-permute-start.20 = (f32[8,1536]{1,0:T(8,128)S(1)}, f32[8,1536]{1,0:T(8,128)S(1)}, u32[]{:S(2)}, u32[]{:S(2)}) collective-permute-start(f32[8,1536]{1,0:T(8,128)S(1)} %fusion), channel_id=1, source_target_pairs={{0,17},{1,18},{2,19},{3,20},{4,21},{5,22},{6,23},{7,24},{8,25},{9,... | collective-permute-start | bytes 147464
  1263.8 65.9 %collective-permute-start.19 = (f32[8,1536]{1,0:T(8,128)S(1)}, f32[8,1536]{1,0:T(8,128)S(1)}, u32[]{:S(2)}, u32[]{:S(2)}) collective-permute-start(f32[8,1536]{1,0:T(8,128)S(1)} %fusion), channel_id=1, source_target_pairs={{0,16},{1,17},{2,18},{3,19},{4,20},{5,21},{6,22},{7,23},{8,24},{9,... | collective-permute-start | bytes 147464
  1277.0 65.9 %collective-permute-start.18 = (f32[8,1536]{1,0:T(8,128)S(1)}, f32[8,1536]{1,0:T(8,128)S(1)}, u32[]{:S(2)}, u32[]{:S(2)}) collective-permute-start(f32[8,1536]{1,0:T(8,128)S(1)} %fusion), channel_id=1, source_target_pairs={{0,15},{1,16},{2,17},{3,18},{4,19},{5,20},{6,21},{7,22},{8,23},{9,... | collective-permute-start | bytes 147464
  1290.1 65.9 %collective-permute-start.17 = (f32[8,1536]{1,0:T(8,128)S(1)}, f32[8,1536]{1,0:T(8,128)S(1)}, u32[]{:S(2)}, u32[]{:S(2)}) collective-permute-start(f32[8,1536]{1,0:T(8,128)S(1)} %fusion), channel_id=1, source_target_pairs={{0,14},{1,15},{2,16},{3,17},{4,18},{5,19},{6,20},{7,21},{8,22},{9,... | collective-permute-start | bytes 147464
  1303.3 65.9 %collective-permute-start.16 = (f32[8,1536]{1,0:T(8,128)S(1)}, f32[8,1536]{1,0:T(8,128)S(1)}, u32[]{:S(2)}, u32[]{:S(2)}) collective-permute-start(f32[8,1536]{1,0:T(8,128)S(1)} %fusion), channel_id=1, source_target_pairs={{0,13},{1,14},{2,15},{3,16},{4,17},{5,18},{6,19},{7,20},{8,21},{9,... | collective-permute-start | bytes 147464
  1316.4 65.9 %collective-permute-start.15 = (f32[8,1536]{1,0:T(8,128)S(1)}, f32[8,1536]{1,0:T(8,128)S(1)}, u32[]{:S(2)}, u32[]{:S(2)}) collective-permute-start(f32[8,1536]{1,0:T(8,128)S(1)} %fusion), channel_id=1, source_target_pairs={{0,12},{1,13},{2,14},{3,15},{4,16},{5,17},{6,18},{7,19},{8,20},{9,... | collective-permute-start | bytes 147464
  1329.7 65.7 %collective-permute-start.14 = (f32[8,1536]{1,0:T(8,128)S(1)}, f32[8,1536]{1,0:T(8,128)S(1)}, u32[]{:S(2)}, u32[]{:S(2)}) collective-permute-start(f32[8,1536]{1,0:T(8,128)S(1)} %fusion), channel_id=1, source_target_pairs={{0,11},{1,12},{2,13},{3,14},{4,15},{5,16},{6,17},{7,18},{8,19},{9,... | collective-permute-start | bytes 147464
  1342.9 65.7 %collective-permute-start.13 = (f32[8,1536]{1,0:T(8,128)S(1)}, f32[8,1536]{1,0:T(8,128)S(1)}, u32[]{:S(2)}, u32[]{:S(2)}) collective-permute-start(f32[8,1536]{1,0:T(8,128)S(1)} %fusion), channel_id=1, source_target_pairs={{0,10},{1,11},{2,12},{3,13},{4,14},{5,15},{6,16},{7,17},{8,18},{9,... | collective-permute-start | bytes 147464
  1356.0 66.3 %collective-permute-start.12 = (f32[8,1536]{1,0:T(8,128)S(1)}, f32[8,1536]{1,0:T(8,128)S(1)}, u32[]{:S(2)}, u32[]{:S(2)}) collective-permute-start(f32[8,1536]{1,0:T(8,128)S(1)} %fusion), channel_id=1, source_target_pairs={{0,9},{1,10},{2,11},{3,12},{4,13},{5,14},{6,15},{7,16},{8,17},{9,1... | collective-permute-start | bytes 147464
  1369.2 66.3 %collective-permute-start.11 = (f32[8,1536]{1,0:T(8,128)S(1)}, f32[8,1536]{1,0:T(8,128)S(1)}, u32[]{:S(2)}, u32[]{:S(2)}) collective-permute-start(f32[8,1536]{1,0:T(8,128)S(1)} %fusion), channel_id=1, source_target_pairs={{0,8},{1,9},{2,10},{3,11},{4,12},{5,13},{6,14},{7,15},{8,16},{9,17... | collective-permute-start | bytes 147464
  1382.3 66.3 %collective-permute-start.10 = (f32[8,1536]{1,0:T(8,128)S(1)}, f32[8,1536]{1,0:T(8,128)S(1)}, u32[]{:S(2)}, u32[]{:S(2)}) collective-permute-start(f32[8,1536]{1,0:T(8,128)S(1)} %fusion), channel_id=1, source_target_pairs={{0,7},{1,8},{2,9},{3,10},{4,11},{5,12},{6,13},{7,14},{8,15},{9,16}... | collective-permute-start | bytes 147464
  1395.5 66.3 %collective-permute-start.9 = (f32[8,1536]{1,0:T(8,128)S(1)}, f32[8,1536]{1,0:T(8,128)S(1)}, u32[]{:S(2)}, u32[]{:S(2)}) collective-permute-start(f32[8,1536]{1,0:T(8,128)S(1)} %fusion), channel_id=1, source_target_pairs={{0,6},{1,7},{2,8},{3,9},{4,10},{5,11},{6,12},{7,13},{8,14},{9,15},... | collective-permute-start | bytes 147464
  1408.6 56.6 %collective-permute-start.8 = (f32[8,1536]{1,0:T(8,128)S(1)}, f32[8,1536]{1,0:T(8,128)}, u32[]{:S(2)}, u32[]{:S(2)}) collective-permute-start(f32[8,1536]{1,0:T(8,128)S(1)} %fusion), channel_id=1, source_target_pairs={{0,5},{1,6},{2,7},{3,8},{4,9},{5,10},{6,11},{7,12},{8,13},{9,14},{... | collective-permute-start | bytes 147464
  1422.4 42.8 %collective-permute-start.7 = (f32[8,1536]{1,0:T(8,128)S(1)}, f32[8,1536]{1,0:T(8,128)}, u32[]{:S(2)}, u32[]{:S(2)}) collective-permute-start(f32[8,1536]{1,0:T(8,128)S(1)} %fusion), channel_id=1, source_target_pairs={{0,4},{1,5},{2,6},{3,7},{4,8},{5,9},{6,10},{7,11},{8,12},{9,13},{1... | collective-permute-start | bytes 147464
  1435.5 29.7 %collective-permute-start.6 = (f32[8,1536]{1,0:T(8,128)S(1)}, f32[8,1536]{1,0:T(8,128)}, u32[]{:S(2)}, u32[]{:S(2)}) collective-permute-start(f32[8,1536]{1,0:T(8,128)S(1)} %fusion), channel_id=1, source_target_pairs={{0,3},{1,4},{2,5},{3,6},{4,7},{5,8},{6,9},{7,10},{8,11},{9,12},{10... | collective-permute-start | bytes 147464
  1448.7 16.5 collective-permute-start.5
  (110 other events, 11059.4 us)
Sparse Core Ops, SparseCore 0:
  11.9 120.5 all-gather.3
  1678.2 246.9 all-reduce.7
where the time goes:
time: 1950 us; the launch traced here: 1930 us
  blocking collectives  1010 us (52%)
  starting transfers between devices  502 us (26%)
  waiting for transfers between devices  239 us (12%)
  local copies, waits for them, and re-layouts  129 us (7%)
  other arithmetic  27.6 us (1%)
    unnamed x1, blocking collectives  710 us
    unnamed x65, starting transfers between devices  489 us
    unnamed x67, waiting for transfers between devices  239 us
    unnamed x183, local copies, waits for them, and re-layouts  109 us
    psum x1, blocking collectives, local(): lax.psum((jnp.sum(grad_pre * normed, axis=0), jnp.sum(grad_pre, axis=0)),...  79.5 us
    psum x1, blocking collectives, local(): lax.psum((jnp.sum(weight_col * conv, axis=0), jnp.sum(weight_col)), ('dp'...  75.7 us
    psum x1, blocking collectives, local(): lax.psum(jnp.sum(weight_col * centred * centred, axis=0), ('dp', 'pair'))  74.2 us
    all_gather x1, blocking collectives, local(): params_full = lax.all_gather(stacked, ('dp', 'pair'), axis=1, tiled=True)  68 us
  transfers between devices with their start and end apart: 70, of which 3 were waited for; matrix products, arithmetic and copies ran while one was open for 44% of the time, Pallas kernels for 0%

commit v1 on v0

--- a/solution.py
+++ b/solution.py
@@ -66,7 +66,7 @@
     )
     grad_pre = weight_col * grad_act * sig * (1.0 + pre * (1.0 - sig))
     scale_sum, shift_sum = lax.psum(
-        (jnp.sum(grad_pre * normed, axis=0), jnp.sum(grad_pre, axis=0)), ("dp", "pair")
+        lax.psum((jnp.sum(grad_pre * normed, axis=0), jnp.sum(grad_pre, axis=0)), "dp"), "pair"
     )
     col_start = device_pos * shard_cols
     grad_scale = lax.dynamic_slice_in_dim(scale_sum, col_start, shard_cols)

time: 1950 us -> 2580 us (1.32)
  blocking collectives: 1010 us -> 1620 us
    psum x1, blocking collectives: 79.5 us -> 579 us  [local(): lax.psum((jnp.sum(grad_pre * normed, axis=0), jnp.sum(grad_pre, axis=0)),...]
    psum x0 -> x1, blocking collectives: none -> 115 us  [local(): lax.psum(lax.psum((jnp.sum(grad_pre * normed, axis=0), jnp.sum(grad_pre,...]
  transfers between devices with their start and end apart: 70 -> 70, of which waited for: 3 -> 3; matrix products, arithmetic and copies ran while one was open for 44% -> 33% of each run, Pallas kernels for 0% -> 0%
where the time goes in v1:
time: 2580 us; the launch traced here: 2570 us
  blocking collectives  1620 us (63%)
  starting transfers between devices  524 us (20%)
  waiting for transfers between devices  235 us (9%)
  local copies, waits for them, and re-layouts  129 us (5%)
  other arithmetic  27.6 us (1%)
    unnamed x1, blocking collectives  710 us
    psum x1, blocking collectives, local(): lax.psum((jnp.sum(grad_pre * normed, axis=0), jnp.sum(grad_pre, axis=0)),...  579 us
    unnamed x65, starting transfers between devices  512 us
    unnamed x67, waiting for transfers between devices  235 us
    psum x1, blocking collectives, local(): lax.psum(lax.psum((jnp.sum(grad_pre * normed, axis=0), jnp.sum(grad_pre,...  115 us
    unnamed x183, local copies, waits for them, and re-layouts  109 us
    psum x1, blocking collectives, local(): lax.psum((jnp.sum(weight_col * conv, axis=0), jnp.sum(weight_col)), ('dp'...  75.7 us
    psum x1, blocking collectives, local(): lax.psum(jnp.sum(weight_col * centred * centred, axis=0), ('dp', 'pair'))  74.2 us
  transfers between devices with their start and end apart: 70, of which 3 were waited for; matrix products, arithmetic and copies ran while one was open for 33% of the time, Pallas kernels for 0%

profile of v1, /device:TPU:1, one launch (start us, length us, event | category | flops | bytes accessed | tf_op | source)
XLA Modules:
  0.0 2566.7 jit_solution(7106529662785749774)
XLA Ops:
  19.3 68.0 %all-gather = f32[256,6,33]{2,1,0:T(8,128)S(1)} all-gather(f32[1,6,33]{2,1,0:T(8,128)S(1)} %maximum_bitcast_fusion), channel_id=1, replica_groups=mesh['dp'=128,'pair'=2] {'dp','pair'}, dimensions={0}, use_global_device_ids=true | all-gather | bytes 203544 | tf_op jit(solution)/shard_map/all_gather | solution.py:35
  88.0 5.6 slice_reduce_fusion.31
  93.6 8.2 slice_reduce_fusion.32
  107.4 75.7 %all-reduce.4 = (f32[1536]{0:T(1024)S(1)}, f32[]{:T(128)}) all-reduce(f32[1536]{0:T(1024)S(1)} %get-tuple-element.91, f32[]{:T(128)} %convert_reduce_fusion), channel_id=1, replica_groups=mesh['dp'=128,'pair'=2] {'dp','pair'}, use_global_device_ids=true, to_apply=%region_1.2 | all-reduce | flops 1537 | bytes 12296 | tf_op jit(solution)/shard_map/psum | solution.py:50
  184.0 74.2 %psum.51 = f32[1536]{0:T(1024)S(1)} all-reduce(f32[1536]{0:T(1024)S(1)} %fusion.119), channel_id=1, replica_groups=mesh['dp'=128,'pair'=2] {'dp','pair'}, use_global_device_ids=true, to_apply=%region_5.6 | all-reduce | flops 1536 | bytes 12288 | tf_op jit(solution)/shard_map/psum | solution.py:55
  258.8 5.2 fusion.124
  264.0 709.9 %fusion = f32[8,1536]{1,0:T(8,128)S(1)} fusion(f32[1536,1536]{1,0:T(8,128)} %fusion.124), kind=kCustom, calls=%all-reduce-scatter | all-reduce-scatter fusion | flops 3145729 | bytes 9486336
  978.8 11.0 collective-permute-start.67
  1005.7 17.9 collective-permute-start.51
  1054.7 8.2 collective-permute-start.37
  1063.0 13.1 collective-permute-start.36
  1076.1 13.1 collective-permute-start.35
  1089.3 13.1 collective-permute-start.34
  1102.4 13.1 collective-permute-start.33
  1115.6 13.1 collective-permute-start.32
  1128.7 13.1 collective-permute-start.31
  1141.9 13.1 collective-permute-start.30
  1155.0 13.1 collective-permute-start.29
  1168.2 13.1 collective-permute-start.28
  1181.3 13.1 collective-permute-start.27
  1194.5 13.1 collective-permute-start.26
  1207.6 13.1 collective-permute-start.25
  1220.8 13.1 collective-permute-start.24
  1233.9 13.1 collective-permute-start.23
  1247.1 13.1 collective-permute-start.22
  1260.2 13.1 collective-permute-start.21
  1273.4 13.1 collective-permute-start.20
  1286.5 13.1 collective-permute-start.19
  1299.7 13.1 collective-permute-start.18
  1312.8 13.1 collective-permute-start.17
  1326.0 13.1 collective-permute-start.16
  1339.1 13.3 collective-permute-start.15
  1352.4 13.1 collective-permute-start.14
  1365.6 13.1 collective-permute-start.13
  1378.7 13.1 collective-permute-start.12
  1391.9 13.1 collective-permute-start.11
  1405.0 13.1 collective-permute-start.10
  1418.2 13.1 collective-permute-start.9
  1431.3 13.7 collective-permute-start.8
  1445.1 13.1 collective-permute-start.7
  1458.2 13.1 collective-permute-start.6
  1471.4 13.1 collective-permute-start.5
  1488.7 97.2 %concatenate.45 = f32[518,1536]{1,0:T(8,128)} concatenate(f32[6,1536]{1,0:T(8,128)S(1)} %collective-permute-done.67, f32[8,1536]{1,0:T(8,128)S(1)} %collective-permute-done.66, f32[8,1536]{1,0:T(8,128)S(1)} %collective-permute-done.65, f32[8,1536]{1,0:T(8,128)S(1)} %collective-permute-done.64, f32[8,1536]{1,0:T(8,128)S(1)} %collective-permute-done.63, ...), dimensions={0} | concatenate | bytes 6365184
  1587.4 8.4 reshape.52
  1602.6 579.3 %all-reduce.5 = (f32[1536]{0:T(1024)S(1)}, f32[1536]{0:T(1024)S(1)}) all-reduce(f32[1536]{0:T(1024)S(1)} %get-tuple-element.50, f32[1536]{0:T(1024)S(1)} %get-tuple-element.49), channel_id=1, replica_groups=mesh['dp'=128,'pair'=2] {'dp'}, use_global_device_ids=true, to_apply=%region_10.11 | all-reduce | flops 3072 | bytes 24576 | tf_op jit(solution)/shard_map/psum | solution.py:69
  2181.9 114.9 %all-reduce.6 = (f32[1536]{0:T(1024)S(1)}, f32[1536]{0:T(1024)S(1)}) all-reduce(f32[1536]{0:T(1024)S(1)} %get-tuple-element.86, f32[1536]{0:T(1024)S(1)} %get-tuple-element.87), channel_id=1, replica_groups=mesh['dp'=128,'pair'=2] {'pair'}, use_global_device_ids=true, to_apply=%region_11.12 | all-reduce | flops 3072 | bytes 24576 | tf_op jit(solution)/shard_map/psum | solution.py:68
  2315.4 9.9 fusion.9
  2325.4 232.7 %all-reduce.9.cloned.1.call-done = f32[31,1536]{1,0:T(8,128)} async-done(((f32[31,1536]{1,0:T(8,128)}), f32[31,1536]{1,0:T(8,128)}) %all-reduce.9.cloned.1.call-update) | async-done | bytes 190480
  (347 shorter events, 102.5 us)
Async XLA Ops:
  7.2 1580.2 %all-gather.4.cloned.1.call-start = ((), (), s32[]{:S(2)}) async-start(), calls=%async_computation | async-start | bytes 6316032 | tf_op jit(solution)/shard_map/all_gather | solution.py:62
  7.9 2550.2 %all-reduce.9.cloned.1.call-start = ((), (), s32[]{:S(2)}) async-start(), calls=%async_computation.1 | async-start | bytes 393216
  9.7 92.7 %collective-permute-start = (bf16[15,1536]{1,0:T(8,128)(2,1)S(1)}, bf16[15,1536]{1,0:T(8,128)(2,1)S(1)}, u32[]{:S(2)}, u32[]{:S(2)}) collective-permute-start(bf16[15,1536]{1,0:T(8,128)(2,1)S(1)} %get-tuple-element.95), channel_id=1, source_target_pairs={{0,1},{1,2},{2,3},{3,4},{4,5},{5,6},{6,7},{7,8},{8,9},{9,10},{10,1... | collective-permute-start | bytes 138248 | tf_op jit(solution)/shard_map/ppermute | solution.py:17
  14.3 88.1 %collective-permute-start.1 = (bf16[15,1536]{1,0:T(8,128)(2,1)S(1)}, bf16[15,1536]{1,0:T(8,128)(2,1)S(1)}, u32[]{:S(2)}, u32[]{:S(2)}) collective-permute-start(bf16[15,1536]{1,0:T(8,128)(2,1)S(1)} %get-tuple-element.96), channel_id=1, source_target_pairs={{1,0},{2,1},{3,2},{4,3},{5,4},{6,5},{7,6},{8,7},{9,8},{10,9},{11,1... | collective-permute-start | bytes 138248 | tf_op jit(solution)/shard_map/ppermute | solution.py:19
  974.0 18.7 collective-permute-start.66
  975.3 18.7 collective-permute-start.65
  977.5 17.8 collective-permute-start.64
  1000.5 23.2 collective-permute-start.55
  1001.8 25.0 collective-permute-start.54
  1003.1 25.3 collective-permute-start.53
  1004.4 26.9 %collective-permute-start.52 = (f32[8,1536]{1,0:T(8,128)S(1)}, f32[8,1536]{1,0:T(8,128)S(1)}, u32[]{:S(2)}, u32[]{:S(2)}) collective-permute-start(f32[8,1536]{1,0:T(8,128)S(1)} %fusion), channel_id=1, source_target_pairs={{0,49},{1,50},{2,51},{3,52},{4,53},{5,54},{6,55},{7,56},{8,57},{9,... | collective-permute-start | bytes 147464
  1005.7 29.5 %collective-permute-start.51 = (f32[8,1536]{1,0:T(8,128)S(1)}, f32[8,1536]{1,0:T(8,128)S(1)}, u32[]{:S(2)}, u32[]{:S(2)}) collective-permute-start(f32[8,1536]{1,0:T(8,128)S(1)} %fusion), channel_id=1, source_target_pairs={{0,48},{1,49},{2,50},{3,51},{4,52},{5,53},{6,54},{7,55},{8,56},{9,... | collective-permute-start | bytes 147464
  1044.4 18.5 collective-permute-start.41
  1045.8 30.3 %collective-permute-start.40 = (f32[8,1536]{1,0:T(8,128)S(1)}, f32[8,1536]{1,0:T(8,128)S(1)}, u32[]{:S(2)}, u32[]{:S(2)}) collective-permute-start(f32[8,1536]{1,0:T(8,128)S(1)} %fusion), channel_id=1, source_target_pairs={{0,37},{1,38},{2,39},{3,40},{4,41},{5,42},{6,43},{7,44},{8,45},{9,... | collective-permute-start | bytes 147464
  1048.6 40.7 %collective-permute-start.39 = (f32[8,1536]{1,0:T(8,128)S(1)}, f32[8,1536]{1,0:T(8,128)S(1)}, u32[]{:S(2)}, u32[]{:S(2)}) collective-permute-start(f32[8,1536]{1,0:T(8,128)S(1)} %fusion), channel_id=1, source_target_pairs={{0,36},{1,37},{2,38},{3,39},{4,40},{5,41},{6,42},{7,43},{8,44},{9,... | collective-permute-start | bytes 147464
  1052.2 50.2 %collective-permute-start.38 = (f32[8,1536]{1,0:T(8,128)S(1)}, f32[8,1536]{1,0:T(8,128)S(1)}, u32[]{:S(2)}, u32[]{:S(2)}) collective-permute-start(f32[8,1536]{1,0:T(8,128)S(1)} %fusion), channel_id=1, source_target_pairs={{0,35},{1,36},{2,37},{3,38},{4,39},{5,40},{6,41},{7,42},{8,43},{9,... | collective-permute-start | bytes 147464
  1054.7 60.8 %collective-permute-start.37 = (f32[8,1536]{1,0:T(8,128)S(1)}, f32[8,1536]{1,0:T(8,128)S(1)}, u32[]{:S(2)}, u32[]{:S(2)}) collective-permute-start(f32[8,1536]{1,0:T(8,128)S(1)} %fusion), channel_id=1, source_target_pairs={{0,34},{1,35},{2,36},{3,37},{4,38},{5,39},{6,40},{7,41},{8,42},{9,... | collective-permute-start | bytes 147464
  1063.0 65.7 %collective-permute-start.36 = (f32[8,1536]{1,0:T(8,128)S(1)}, f32[8,1536]{1,0:T(8,128)S(1)}, u32[]{:S(2)}, u32[]{:S(2)}) collective-permute-start(f32[8,1536]{1,0:T(8,128)S(1)} %fusion), channel_id=1, source_target_pairs={{0,33},{1,34},{2,35},{3,36},{4,37},{5,38},{6,39},{7,40},{8,41},{9,... | collective-permute-start | bytes 147464
  1076.1 65.7 %collective-permute-start.35 = (f32[8,1536]{1,0:T(8,128)S(1)}, f32[8,1536]{1,0:T(8,128)S(1)}, u32[]{:S(2)}, u32[]{:S(2)}) collective-permute-start(f32[8,1536]{1,0:T(8,128)S(1)} %fusion), channel_id=1, source_target_pairs={{0,32},{1,33},{2,34},{3,35},{4,36},{5,37},{6,38},{7,39},{8,40},{9,... | collective-permute-start | bytes 147464
  1089.3 65.7 %collective-permute-start.34 = (f32[8,1536]{1,0:T(8,128)S(1)}, f32[8,1536]{1,0:T(8,128)S(1)}, u32[]{:S(2)}, u32[]{:S(2)}) collective-permute-start(f32[8,1536]{1,0:T(8,128)S(1)} %fusion), channel_id=1, source_target_pairs={{0,31},{1,32},{2,33},{3,34},{4,35},{5,36},{6,37},{7,38},{8,39},{9,... | collective-permute-start | bytes 147464
  1102.4 65.7 %collective-permute-start.33 = (f32[8,1536]{1,0:T(8,128)S(1)}, f32[8,1536]{1,0:T(8,128)S(1)}, u32[]{:S(2)}, u32[]{:S(2)}) collective-permute-start(f32[8,1536]{1,0:T(8,128)S(1)} %fusion), channel_id=1, source_target_pairs={{0,30},{1,31},{2,32},{3,33},{4,34},{5,35},{6,36},{7,37},{8,38},{9,... | collective-permute-start | bytes 147464
  1115.6 65.7 %collective-permute-start.32 = (f32[8,1536]{1,0:T(8,128)S(1)}, f32[8,1536]{1,0:T(8,128)S(1)}, u32[]{:S(2)}, u32[]{:S(2)}) collective-permute-start(f32[8,1536]{1,0:T(8,128)S(1)} %fusion), channel_id=1, source_target_pairs={{0,29},{1,30},{2,31},{3,32},{4,33},{5,34},{6,35},{7,36},{8,37},{9,... | collective-permute-start | bytes 147464
  1128.7 65.7 %collective-permute-start.31 = (f32[8,1536]{1,0:T(8,128)S(1)}, f32[8,1536]{1,0:T(8,128)S(1)}, u32[]{:S(2)}, u32[]{:S(2)}) collective-permute-start(f32[8,1536]{1,0:T(8,128)S(1)} %fusion), channel_id=1, source_target_pairs={{0,28},{1,29},{2,30},{3,31},{4,32},{5,33},{6,34},{7,35},{8,36},{9,... | collective-permute-start | bytes 147464
  1141.9 65.7 %collective-permute-start.30 = (f32[8,1536]{1,0:T(8,128)S(1)}, f32[8,1536]{1,0:T(8,128)S(1)}, u32[]{:S(2)}, u32[]{:S(2)}) collective-permute-start(f32[8,1536]{1,0:T(8,128)S(1)} %fusion), channel_id=1, source_target_pairs={{0,27},{1,28},{2,29},{3,30},{4,31},{5,32},{6,33},{7,34},{8,35},{9,... | collective-permute-start | bytes 147464
  1155.0 65.7 %collective-permute-start.29 = (f32[8,1536]{1,0:T(8,128)S(1)}, f32[8,1536]{1,0:T(8,128)S(1)}, u32[]{:S(2)}, u32[]{:S(2)}) collective-permute-start(f32[8,1536]{1,0:T(8,128)S(1)} %fusion), channel_id=1, source_target_pairs={{0,26},{1,27},{2,28},{3,29},{4,30},{5,31},{6,32},{7,33},{8,34},{9,... | collective-permute-start | bytes 147464
  1168.2 65.7 %collective-permute-start.28 = (f32[8,1536]{1,0:T(8,128)S(1)}, f32[8,1536]{1,0:T(8,128)S(1)}, u32[]{:S(2)}, u32[]{:S(2)}) collective-permute-start(f32[8,1536]{1,0:T(8,128)S(1)} %fusion), channel_id=1, source_target_pairs={{0,25},{1,26},{2,27},{3,28},{4,29},{5,30},{6,31},{7,32},{8,33},{9,... | collective-permute-start | bytes 147464
  1181.3 65.7 %collective-permute-start.27 = (f32[8,1536]{1,0:T(8,128)S(1)}, f32[8,1536]{1,0:T(8,128)S(1)}, u32[]{:S(2)}, u32[]{:S(2)}) collective-permute-start(f32[8,1536]{1,0:T(8,128)S(1)} %fusion), channel_id=1, source_target_pairs={{0,24},{1,25},{2,26},{3,27},{4,28},{5,29},{6,30},{7,31},{8,32},{9,... | collective-permute-start | bytes 147464
  1194.5 65.7 %collective-permute-start.26 = (f32[8,1536]{1,0:T(8,128)S(1)}, f32[8,1536]{1,0:T(8,128)S(1)}, u32[]{:S(2)}, u32[]{:S(2)}) collective-permute-start(f32[8,1536]{1,0:T(8,128)S(1)} %fusion), channel_id=1, source_target_pairs={{0,23},{1,24},{2,25},{3,26},{4,27},{5,28},{6,29},{7,30},{8,31},{9,... | collective-permute-start | bytes 147464
  1207.6 65.7 %collective-permute-start.25 = (f32[8,1536]{1,0:T(8,128)S(1)}, f32[8,1536]{1,0:T(8,128)S(1)}, u32[]{:S(2)}, u32[]{:S(2)}) collective-permute-start(f32[8,1536]{1,0:T(8,128)S(1)} %fusion), channel_id=1, source_target_pairs={{0,22},{1,23},{2,24},{3,25},{4,26},{5,27},{6,28},{7,29},{8,30},{9,... | collective-permute-start | bytes 147464
  1220.8 65.7 %collective-permute-start.24 = (f32[8,1536]{1,0:T(8,128)S(1)}, f32[8,1536]{1,0:T(8,128)S(1)}, u32[]{:S(2)}, u32[]{:S(2)}) collective-permute-start(f32[8,1536]{1,0:T(8,128)S(1)} %fusion), channel_id=1, source_target_pairs={{0,21},{1,22},{2,23},{3,24},{4,25},{5,26},{6,27},{7,28},{8,29},{9,... | collective-permute-start | bytes 147464
  1233.9 65.7 %collective-permute-start.23 = (f32[8,1536]{1,0:T(8,128)S(1)}, f32[8,1536]{1,0:T(8,128)S(1)}, u32[]{:S(2)}, u32[]{:S(2)}) collective-permute-start(f32[8,1536]{1,0:T(8,128)S(1)} %fusion), channel_id=1, source_target_pairs={{0,20},{1,21},{2,22},{3,23},{4,24},{5,25},{6,26},{7,27},{8,28},{9,... | collective-permute-start | bytes 147464
  1247.1 65.7 %collective-permute-start.22 = (f32[8,1536]{1,0:T(8,128)S(1)}, f32[8,1536]{1,0:T(8,128)S(1)}, u32[]{:S(2)}, u32[]{:S(2)}) collective-permute-start(f32[8,1536]{1,0:T(8,128)S(1)} %fusion), channel_id=1, source_target_pairs={{0,19},{1,20},{2,21},{3,22},{4,23},{5,24},{6,25},{7,26},{8,27},{9,... | collective-permute-start | bytes 147464
  1260.2 65.7 %collective-permute-start.21 = (f32[8,1536]{1,0:T(8,128)S(1)}, f32[8,1536]{1,0:T(8,128)S(1)}, u32[]{:S(2)}, u32[]{:S(2)}) collective-permute-start(f32[8,1536]{1,0:T(8,128)S(1)} %fusion), channel_id=1, source_target_pairs={{0,18},{1,19},{2,20},{3,21},{4,22},{5,23},{6,24},{7,25},{8,26},{9,... | collective-permute-start | bytes 147464
  1273.4 65.7 %collective-permute-start.20 = (f32[8,1536]{1,0:T(8,128)S(1)}, f32[8,1536]{1,0:T(8,128)S(1)}, u32[]{:S(2)}, u32[]{:S(2)}) collective-permute-start(f32[8,1536]{1,0:T(8,128)S(1)} %fusion), channel_id=1, source_target_pairs={{0,17},{1,18},{2,19},{3,20},{4,21},{5,22},{6,23},{7,24},{8,25},{9,... | collective-permute-start | bytes 147464
  1286.5 65.9 %collective-permute-start.19 = (f32[8,1536]{1,0:T(8,128)S(1)}, f32[8,1536]{1,0:T(8,128)S(1)}, u32[]{:S(2)}, u32[]{:S(2)}) collective-permute-start(f32[8,1536]{1,0:T(8,128)S(1)} %fusion), channel_id=1, source_target_pairs={{0,16},{1,17},{2,18},{3,19},{4,20},{5,21},{6,22},{7,23},{8,24},{9,... | collective-permute-start | bytes 147464
  1299.7 65.9 %collective-permute-start.18 = (f32[8,1536]{1,0:T(8,128)S(1)}, f32[8,1536]{1,0:T(8,128)S(1)}, u32[]{:S(2)}, u32[]{:S(2)}) collective-permute-start(f32[8,1536]{1,0:T(8,128)S(1)} %fusion), channel_id=1, source_target_pairs={{0,15},{1,16},{2,17},{3,18},{4,19},{5,20},{6,21},{7,22},{8,23},{9,... | collective-permute-start | bytes 147464
  1312.8 65.9 %collective-permute-start.17 = (f32[8,1536]{1,0:T(8,128)S(1)}, f32[8,1536]{1,0:T(8,128)S(1)}, u32[]{:S(2)}, u32[]{:S(2)}) collective-permute-start(f32[8,1536]{1,0:T(8,128)S(1)} %fusion), channel_id=1, source_target_pairs={{0,14},{1,15},{2,16},{3,17},{4,18},{5,19},{6,20},{7,21},{8,22},{9,... | collective-permute-start | bytes 147464
  1326.0 65.9 %collective-permute-start.16 = (f32[8,1536]{1,0:T(8,128)S(1)}, f32[8,1536]{1,0:T(8,128)S(1)}, u32[]{:S(2)}, u32[]{:S(2)}) collective-permute-start(f32[8,1536]{1,0:T(8,128)S(1)} %fusion), channel_id=1, source_target_pairs={{0,13},{1,14},{2,15},{3,16},{4,17},{5,18},{6,19},{7,20},{8,21},{9,... | collective-permute-start | bytes 147464
  1339.1 65.9 %collective-permute-start.15 = (f32[8,1536]{1,0:T(8,128)S(1)}, f32[8,1536]{1,0:T(8,128)S(1)}, u32[]{:S(2)}, u32[]{:S(2)}) collective-permute-start(f32[8,1536]{1,0:T(8,128)S(1)} %fusion), channel_id=1, source_target_pairs={{0,12},{1,13},{2,14},{3,15},{4,16},{5,17},{6,18},{7,19},{8,20},{9,... | collective-permute-start | bytes 147464
  1352.4 65.7 %collective-permute-start.14 = (f32[8,1536]{1,0:T(8,128)S(1)}, f32[8,1536]{1,0:T(8,128)S(1)}, u32[]{:S(2)}, u32[]{:S(2)}) collective-permute-start(f32[8,1536]{1,0:T(8,128)S(1)} %fusion), channel_id=1, source_target_pairs={{0,11},{1,12},{2,13},{3,14},{4,15},{5,16},{6,17},{7,18},{8,19},{9,... | collective-permute-start | bytes 147464
  1365.6 65.7 %collective-permute-start.13 = (f32[8,1536]{1,0:T(8,128)S(1)}, f32[8,1536]{1,0:T(8,128)S(1)}, u32[]{:S(2)}, u32[]{:S(2)}) collective-permute-start(f32[8,1536]{1,0:T(8,128)S(1)} %fusion), channel_id=1, source_target_pairs={{0,10},{1,11},{2,12},{3,13},{4,14},{5,15},{6,16},{7,17},{8,18},{9,... | collective-permute-start | bytes 147464
  1378.7 66.3 %collective-permute-start.12 = (f32[8,1536]{1,0:T(8,128)S(1)}, f32[8,1536]{1,0:T(8,128)S(1)}, u32[]{:S(2)}, u32[]{:S(2)}) collective-permute-start(f32[8,1536]{1,0:T(8,128)S(1)} %fusion), channel_id=1, source_target_pairs={{0,9},{1,10},{2,11},{3,12},{4,13},{5,14},{6,15},{7,16},{8,17},{9,1... | collective-permute-start | bytes 147464
  1391.9 66.3 %collective-permute-start.11 = (f32[8,1536]{1,0:T(8,128)S(1)}, f32[8,1536]{1,0:T(8,128)S(1)}, u32[]{:S(2)}, u32[]{:S(2)}) collective-permute-start(f32[8,1536]{1,0:T(8,128)S(1)} %fusion), channel_id=1, source_target_pairs={{0,8},{1,9},{2,10},{3,11},{4,12},{5,13},{6,14},{7,15},{8,16},{9,17... | collective-permute-start | bytes 147464
  1405.0 66.3 %collective-permute-start.10 = (f32[8,1536]{1,0:T(8,128)S(1)}, f32[8,1536]{1,0:T(8,128)S(1)}, u32[]{:S(2)}, u32[]{:S(2)}) collective-permute-start(f32[8,1536]{1,0:T(8,128)S(1)} %fusion), channel_id=1, source_target_pairs={{0,7},{1,8},{2,9},{3,10},{4,11},{5,12},{6,13},{7,14},{8,15},{9,16}... | collective-permute-start | bytes 147464
  1418.2 66.3 %collective-permute-start.9 = (f32[8,1536]{1,0:T(8,128)S(1)}, f32[8,1536]{1,0:T(8,128)S(1)}, u32[]{:S(2)}, u32[]{:S(2)}) collective-permute-start(f32[8,1536]{1,0:T(8,128)S(1)} %fusion), channel_id=1, source_target_pairs={{0,6},{1,7},{2,8},{3,9},{4,10},{5,11},{6,12},{7,13},{8,14},{9,15},... | collective-permute-start | bytes 147464
  1431.3 56.6 %collective-permute-start.8 = (f32[8,1536]{1,0:T(8,128)S(1)}, f32[8,1536]{1,0:T(8,128)}, u32[]{:S(2)}, u32[]{:S(2)}) collective-permute-start(f32[8,1536]{1,0:T(8,128)S(1)} %fusion), channel_id=1, source_target_pairs={{0,5},{1,6},{2,7},{3,8},{4,9},{5,10},{6,11},{7,12},{8,13},{9,14},{... | collective-permute-start | bytes 147464
  1445.1 42.8 %collective-permute-start.7 = (f32[8,1536]{1,0:T(8,128)S(1)}, f32[8,1536]{1,0:T(8,128)}, u32[]{:S(2)}, u32[]{:S(2)}) collective-permute-start(f32[8,1536]{1,0:T(8,128)S(1)} %fusion), channel_id=1, source_target_pairs={{0,4},{1,5},{2,6},{3,7},{4,8},{5,9},{6,10},{7,11},{8,12},{9,13},{1... | collective-permute-start | bytes 147464
  1458.2 29.7 %collective-permute-start.6 = (f32[8,1536]{1,0:T(8,128)S(1)}, f32[8,1536]{1,0:T(8,128)}, u32[]{:S(2)}, u32[]{:S(2)}) collective-permute-start(f32[8,1536]{1,0:T(8,128)S(1)} %fusion), channel_id=1, source_target_pairs={{0,3},{1,4},{2,5},{3,6},{4,7},{5,8},{6,9},{7,10},{8,11},{9,12},{10... | collective-permute-start | bytes 147464
  (110 other events, 16142.0 us)
Sparse Core Ops, SparseCore 0:
  11.9 120.5 all-gather.3
  2315.5 242.5 all-reduce.8
